TPU v7x, 32 devices: a whole 2x2x4 slice. The times are simulated.
32 devices in a mesh: rep: 2 (over y), ep: 4 (over x, core), et: 4 (over z).
Axes of the slice: x: 2, y: 2, z: 4, core: 2. Of those that a mesh axis runs over, the one named last changes fastest.
Arguments:
- tokens: bfloat16 [1024, 3072], P(('rep', 'ep'), 'et'), parts along dimension 0, may hold values from -6 to 6
- out_grad: bfloat16 [1024, 3072], P(('rep', 'ep'), 'et'), parts along dimension 0, may hold values from -6 to 6
- route_ids: int32 [1024, 2], P(('rep', 'ep')), parts along dimension 0, may hold values from 0 to 3, all different within a row; in each aligned block of 128 rows (0 to 127, 128 to 255, ...) at most 72 rows name the same one
- route_weight: bfloat16 [1024, 2], P(('rep', 'ep')), parts along dimension 0, may hold values from 0.049804688 to 1
- w_gate: bfloat16 [3072, 32768], P(None, ('ep', 'et')), may hold values from -0.109375 to 0.109375
- w_up: bfloat16 [3072, 32768], P(None, ('ep', 'et')), may hold values from -0.109375 to 0.109375
- w_down: bfloat16 [32768, 3072], P(('ep', 'et')), may hold values from -0.0625 to 0.0625
Outputs:
- token_grad: bfloat16 [1024, 3072], P(('rep', 'ep'), 'et'), parts along dimension 0
- route_grad: float32 [1024, 2], P(('rep', 'ep')), parts along dimension 0
- gate_grad: bfloat16 [6144, 32768], P('rep', ('ep', 'et')), parts along dimension 0
- up_grad: bfloat16 [6144, 32768], P('rep', ('ep', 'et')), parts along dimension 0
- down_grad: bfloat16 [32768, 6144], P(('ep', 'et'), 'rep'), parts along dimension 1
There are 2 independent parts, one for each index of `rep`. A program takes and returns all parts, laid end to end along the dimension named above; an argument that names none is the same for every part. Nothing has to cross between parts.
Inputs may be any that keep to these rules, and one draw needn't show every extreme that they name: `route_ids`: each token names 2 different experts. Among the 128 tokens of one index of ep, no expert is named by more than 72 tokens, and in some such block one expert is named by exactly 72.
All inputs are finite; a program needn't handle non-finite values.
Results may differ from a plain program's by a relative error of at most 0.012.
Values may be sent and summed in bfloat16 or wider, within the bound.
A program may use at most 192 MiB of HBM per device.

v0:
```python
import jax
import jax.numpy as jnp
from jax import lax
from jax.sharding import PartitionSpec as P

EXP = 4
CAP = 72


def routing(route_ids, route_weight):
    expert_range = jnp.arange(EXP, dtype=jnp.int32)
    expert_hit = route_ids[:, :, None] == expert_range[None, None, :]
    token_hit = jnp.any(expert_hit, axis=1).astype(jnp.int32)
    before = jnp.cumsum(token_hit, axis=0) - token_hit
    position = jnp.sum(jnp.where(expert_hit, before[:, None, :], 0), axis=2)
    slot_of = route_ids * CAP + position
    slot_range = jnp.arange(CAP, dtype=jnp.int32)
    placed = (before.T[:, None, :] == slot_range[None, :, None]) & (token_hit.T[:, None, :] > 0)
    token_range = jnp.arange(route_ids.shape[0], dtype=jnp.int32)
    slot_token = jnp.sum(jnp.where(placed, token_range[None, None, :], 0), axis=2)
    filled = jnp.any(placed, axis=2)
    token_weight = jnp.sum(
        jnp.where(expert_hit, route_weight.astype(jnp.float32)[:, :, None], 0.0), axis=1
    )
    picked = jnp.take_along_axis(token_weight.T, slot_token, axis=1)
    slot_weight = jnp.where(filled, picked, 0.0)
    select = placed.astype(jnp.bfloat16).reshape(EXP * CAP, -1)
    return (slot_of, select, slot_weight)


def pack_rows(select_half, source, group):
    flat = jnp.dot(select_half, source, preferred_element_type=jnp.float32).astype(jnp.bfloat16)
    return jnp.repeat(flat.reshape(EXP, CAP, source.shape[1]), group, axis=0)


def unpack_slots(back_rows, back_route, slot_of, group):
    per_expert = jnp.sum(
        back_rows.reshape(EXP, group, CAP, back_rows.shape[2]), axis=1, dtype=jnp.float32
    ).reshape(EXP * CAP, -1)
    token_sum = jnp.sum(per_expert[slot_of], axis=1)
    route_expert = jnp.sum(back_route.reshape(EXP, group, CAP), axis=1, dtype=jnp.float32).reshape(
        EXP * CAP
    )
    route_sum = route_expert[slot_of]
    return (token_sum, route_sum)


def body(tokens, out_grad, route_ids, route_weight, w_gate, w_up, w_down):
    group = lax.axis_size("ep") // EXP
    slot_of, select_half, slot_weight = routing(route_ids, route_weight)
    slot_scale = jnp.repeat(slot_weight.astype(jnp.bfloat16), group, axis=0)
    whole_x, whole_dy = (
        lax.all_gather(tokens, "et", axis=1, tiled=True),
        lax.all_gather(out_grad, "et", axis=1, tiled=True),
    )
    expert_x, expert_dy, recv_scale = (
        lax.all_to_all(
            pack_rows(select_half, whole_x, group), "ep", split_axis=0, concat_axis=0, tiled=True
        ),
        lax.all_to_all(
            pack_rows(select_half, whole_dy, group), "ep", split_axis=0, concat_axis=0, tiled=True
        ),
        lax.all_to_all(slot_scale, "ep", split_axis=0, concat_axis=0, tiled=True),
    )
    senders = expert_x.shape[0]
    width = expert_x.shape[2]
    flat_x = expert_x.reshape(senders * CAP, width)
    flat_dy = expert_dy.reshape(senders * CAP, width)
    scale = recv_scale.reshape(-1).astype(jnp.float32)[:, None]
    contract_rows = (((0,), (0,)), ((), ()))
    contract_hidden = (((1,), (1,)), ((), ()))
    gate = jnp.dot(flat_x, w_gate, preferred_element_type=jnp.float32)
    upper = jnp.dot(flat_x, w_up, preferred_element_type=jnp.float32)
    sigma = jax.nn.sigmoid(gate)
    silu_gate = gate * sigma
    active = silu_gate * upper
    scaled = (scale * active).astype(jnp.bfloat16)
    raw_grad = lax.dot_general(flat_dy, w_down, contract_hidden, preferred_element_type=jnp.float32)
    slot_route = jnp.sum(active * raw_grad, axis=1).astype(jnp.bfloat16)
    hidden_grad = scale * raw_grad
    gate_delta = (hidden_grad * upper * sigma * (1.0 + gate * (1.0 - sigma))).astype(jnp.bfloat16)
    up_delta = (hidden_grad * silu_gate).astype(jnp.bfloat16)
    gate_grad = lax.dot_general(
        flat_x, gate_delta, contract_rows, preferred_element_type=jnp.float32
    ).astype(jnp.bfloat16)
    up_grad = lax.dot_general(
        flat_x, up_delta, contract_rows, preferred_element_type=jnp.float32
    ).astype(jnp.bfloat16)
    down_grad = lax.dot_general(
        scaled, flat_dy, contract_rows, preferred_element_type=jnp.float32
    ).astype(jnp.bfloat16)
    token_part = lax.dot_general(
        gate_delta, w_gate, contract_hidden, preferred_element_type=jnp.float32
    )
    token_part = token_part + lax.dot_general(
        up_delta, w_up, contract_hidden, preferred_element_type=jnp.float32
    )
    token_half = token_part.astype(jnp.bfloat16)
    back_rows, back_route = (
        lax.all_to_all(
            token_half.reshape(senders, CAP, width), "ep", split_axis=0, concat_axis=0, tiled=True
        ),
        lax.all_to_all(
            slot_route.reshape(senders, CAP), "ep", split_axis=0, concat_axis=0, tiled=True
        ),
    )
    token_sum, route_sum = unpack_slots(back_rows, back_route, slot_of, group)
    token_grad = lax.psum_scatter(
        token_sum.astype(jnp.bfloat16), "et", scatter_dimension=1, tiled=True
    )
    route_grad = lax.psum(route_sum, "et")
    return (token_grad, route_grad, gate_grad, up_grad, down_grad)


def solution(mesh):
    return jax.shard_map(
        body,
        mesh=mesh,
        in_specs=(
            P(("rep", "ep"), "et"),
            P(("rep", "ep"), "et"),
            P(("rep", "ep"), None),
            P(("rep", "ep"), None),
            P(None, ("ep", "et")),
            P(None, ("ep", "et")),
            P(("ep", "et"), None),
        ),
        out_specs=(
            P(("rep", "ep"), "et"),
            P(("rep", "ep"), None),
            P("rep", ("ep", "et")),
            P("rep", ("ep", "et")),
            P(("ep", "et"), "rep"),
        ),
        check_vma=False,
    )
```

profile of v0, /device:TPU:0, one launch (start us, length us, event | category | flops | bytes accessed | tf_op | source)
XLA Modules:
  0.0 218.9 jit_solution(4287822480476246712)
XLA Ops:
  10.1 3.1 %gather_fusion.2 = bf16[288]{0:T(512)(128)(2,1)S(1)} fusion(bf16[4,128]{0,1:T(8,128)(2,1)S(1)} %bitcast.47, s32[288]{0:T(512)S(1)} %reshape.168), kind=kCustom, calls=%fused_computation.2 | custom fusion | bytes 3456 | tf_op jit(solution)/shard_map/jit(take_along_axis)/gather | solution.py:25
  13.9 4.2 %all-to-all-start = ((bf16[4,1,72]{2,1,0:T(2,128)(2,1)}), bf16[4,1,72]{2,1,0:T(2,128)(2,1)S(1)}, u32[]{:S(2)}, u32[]{:S(2)}) async-start(bf16[4,1,72]{2,1,0:T(2,128)(2,1)} %copy.52), calls=%async_computation | async-start | bytes 4096 | tf_op jit(solution)/shard_map/all_to_all | solution.py:63
  18.3 20.5 %all_gather.7 = bf16[128,3072]{1,0:T(8,128)(2,1)S(1)} all-gather(bf16[128,768]{1,0:T(8,128)(2,1)} %param.7), channel_id=1, replica_groups=mesh['rep'=2,'ep'=4,'et'=4] {'et'}, dimensions={1}, use_global_device_ids=true | all-gather | bytes 983040 | tf_op jit(solution)/shard_map/all_gather | solution.py:53
  40.7 3.7 %all-to-all-start.2 = ((bf16[4,72,3072]{2,1,0:T(8,128)(2,1)}), bf16[4,72,3072]{2,1,0:T(8,128)(2,1)S(1)}, u32[]{:S(2)}, u32[]{:S(2)}) async-start(bf16[4,72,3072]{2,1,0:T(8,128)(2,1)} %bitcast.10), calls=%async_computation.2 | async-start | bytes 3538944 | tf_op jit(solution)/shard_map/all_to_all | solution.py:57
  44.7 18.1 %all_gather.6 = bf16[128,3072]{1,0:T(8,128)(2,1)S(1)} all-gather(bf16[128,768]{1,0:T(8,128)(2,1)S(1)} %copy-done.2), channel_id=1, replica_groups=mesh['rep'=2,'ep'=4,'et'=4] {'et'}, dimensions={1}, use_global_device_ids=true | all-gather | bytes 983040 | tf_op jit(solution)/shard_map/all_gather | solution.py:54
  66.5 3.8 %all-to-all-start.1 = ((bf16[4,72,3072]{2,1,0:T(8,128)(2,1)}), bf16[4,72,3072]{2,1,0:T(8,128)(2,1)S(1)}, u32[]{:S(2)}, u32[]{:S(2)}) async-start(bf16[4,72,3072]{2,1,0:T(8,128)(2,1)} %bitcast.8), calls=%async_computation.1 | async-start | bytes 3538944 | tf_op jit(solution)/shard_map/all_to_all | solution.py:60
  70.3 8.3 %fusion.13 = f32[288,2048]{1,0:T(8,128)} fusion(bf16[288,3072]{1,0:T(8,128)(2,1)S(1)} %bitcast.48, bf16[3072,2048]{1,0:T(8,128)(2,1)} %param.11), kind=kOutput, calls=%fused_computation.42 | convolution fusion | flops 3623878656 | bytes 16711680 | tf_op jit(solution)/shard_map/dot_general | solution.py:72
  78.6 8.3 %fusion.12 = f32[288,2048]{1,0:T(8,128)} fusion(bf16[288,3072]{1,0:T(8,128)(2,1)S(1)} %bitcast.49, bf16[3072,2048]{1,0:T(8,128)(2,1)} %param.12), kind=kOutput, calls=%fused_computation.41 | convolution fusion | flops 3623878656 | bytes 16711680 | tf_op jit(solution)/shard_map/dot_general | solution.py:73
  86.8 5.4 %all-to-all-done.1 = bf16[4,72,3072]{2,1,0:T(8,128)(2,1)S(1)} async-done(((bf16[4,72,3072]{2,1,0:T(8,128)(2,1)}), bf16[4,72,3072]{2,1,0:T(8,128)(2,1)S(1)}, u32[]{:S(2)}, u32[]{:S(2)}) %all-to-all-start.1) | async-done | bytes 1769504 | tf_op jit(solution)/shard_map/all_to_all | solution.py:60
  92.3 10.8 %multiply_reduce_fusion = (bf16[288]{0:T(512)(128)(2,1)S(1)}, bf16[288,2048]{1,0:T(8,128)(2,1)S(1)}, bf16[288,2048]{1,0:T(8,128)(2,1)S(1)}) fusion(f32[288,2048]{1,0:T(8,128)} %fusion.12, f32[288,2048]{1,0:T(8,128)} %fusion.13, f32[288]{0:T(512)S(1)} %reshape.147, bf16[288,3072]{1,0:T(8,128)(2,1)S(1)} %bitcast.52, bf16[2048,3072]{1,0:T(8,128)(2,1)} %param.13), kind=kOutput, calls=%fused_computation.11 | convolution fusion | flops 3633905408 | bytes 21432000 | tf_op jit(solution)/shard_map/dot_general | solution.py:78
  103.0 7.7 %fusion.14 = f32[288,3072]{1,0:T(8,128)S(1)} fusion(bf16[288,2048]{1,0:T(8,128)(2,1)S(1)} %get-tuple-element.31, bf16[3072,2048]{1,0:T(8,128)(2,1)} %param.11), kind=kOutput, calls=%fused_computation.43 | convolution fusion | flops 3623878656 | bytes 17301504 | tf_op jit(solution)/shard_map/dot_general | solution.py:92
  110.8 14.2 %fusion = bf16[288,3072]{1,0:T(8,128)(2,1)} fusion(f32[288,3072]{1,0:T(8,128)S(1)} %fusion.14, bf16[288,2048]{1,0:T(8,128)(2,1)S(1)} %get-tuple-element.32, bf16[3072,2048]{1,0:T(8,128)(2,1)} %param.12), kind=kOutput, calls=%fused_computation.7 | convolution fusion | flops 3625648128 | bytes 19070976 | tf_op jit(solution)/shard_map/dot_general | solution.py:95
  125.0 4.4 %all-to-all-start.3 = ((bf16[4,72,3072]{2,1,0:T(8,128)(2,1)}), bf16[4,72,3072]{2,1,0:T(8,128)(2,1)}, u32[]{:S(2)}, u32[]{:S(2)}) async-start(bf16[4,72,3072]{2,1,0:T(8,128)(2,1)} %bitcast.12), calls=%async_computation.3 | async-start | bytes 3538944 | tf_op jit(solution)/shard_map/all_to_all | solution.py:100
  129.4 12.6 %convolution_convert_fusion = bf16[2048,3072]{1,0:T(8,128)(2,1)} fusion(bf16[288,3072]{1,0:T(8,128)(2,1)S(1)} %bitcast.53, f32[288]{0:T(512)S(1)} %reshape.147, f32[288,2048]{1,0:T(8,128)} %fusion.12, f32[288,2048]{1,0:T(8,128)} %fusion.13), kind=kOutput, calls=%fused_computation.3 | convolution fusion | flops 3634298880 | bytes 19072128 | tf_op jit(solution)/shard_map/dot_general | solution.py:89
  142.1 9.6 %all-to-all-done.3 = bf16[4,72,3072]{2,1,0:T(8,128)(2,1)} async-done(((bf16[4,72,3072]{2,1,0:T(8,128)(2,1)}), bf16[4,72,3072]{2,1,0:T(8,128)(2,1)}, u32[]{:S(2)}, u32[]{:S(2)}) %all-to-all-start.3) | async-done | bytes 1769504 | tf_op jit(solution)/shard_map/all_to_all | solution.py:100
  151.6 1.9 bitcast_convert_fusion
  153.5 3.3 %gather_fusion = f32[256,3072]{1,0:T(8,128)} fusion(f32[288,3072]{1,0:T(8,128)S(1)} %bitcast_convert_fusion, s32[1024]{0:T(1024)S(1)} %pad_clamp_fusion), kind=kCustom, calls=%fused_computation | custom fusion | bytes 6292480 | tf_op jit(solution)/shard_map/gather | solution.py:40
  156.9 3.7 %reshape.157 = f32[128,2,3072]{2,1,0:T(2,128)S(1)} reshape(f32[256,3072]{1,0:T(8,128)} %gather_fusion) | data formatting | bytes 6291456 | tf_op jit(solution)/shard_map/gather | solution.py:40
  160.6 5.2 %reduce_sum.62 = bf16[128,3072]{1,0:T(8,128)(2,1)} reduce(f32[128,2,3072]{2,1,0:T(2,128)S(1)} %reshape.157, f32[]{:T(128)} %constant.13.clone.1), dimensions={1}, to_apply=%region_6.7 | reduce | flops 393216 | bytes 3932164 | tf_op jit(solution)/shard_map/reduce_sum | solution.py:40
  165.8 11.6 %convolution_convert_fusion.1 = bf16[3072,2048]{1,0:T(8,128)(2,1)} fusion(bf16[288,3072]{1,0:T(8,128)(2,1)} %bitcast.50, bf16[288,2048]{1,0:T(8,128)(2,1)} %copy-done.4), kind=kOutput, calls=%fused_computation.4 | convolution fusion | flops 3630170112 | bytes 15532032 | tf_op jit(solution)/shard_map/dot_general | solution.py:86
  178.1 3.2 %all-to-all-start.4 = ((bf16[4,1,72]{2,1,0:T(2,128)(2,1)}), bf16[4,1,72]{2,1,0:T(2,128)(2,1)S(1)}, u32[]{:S(2)}, u32[]{:S(2)}) async-start(bf16[4,1,72]{2,1,0:T(2,128)(2,1)} %convert_element_type.101), calls=%async_computation.5 | async-start | bytes 4096 | tf_op jit(solution)/shard_map/all_to_all | solution.py:103
  181.3 9.7 %convolution_convert_fusion.2 = bf16[3072,2048]{1,0:T(8,128)(2,1)} fusion(bf16[288,3072]{1,0:T(8,128)(2,1)S(1)} %bitcast.51, bf16[288,2048]{1,0:T(8,128)(2,1)S(1)} %copy-done.6), kind=kOutput, calls=%fused_computation.5 | convolution fusion | flops 3630170112 | bytes 15532032 | tf_op jit(solution)/shard_map/dot_general | solution.py:83
  191.1 1.9 gather_fusion.1
  193.2 18.2 %psum.7 = f32[128,2]{1,0:T(8,128)S(1)} all-reduce(f32[128,2]{1,0:T(8,128)S(1)} %reshape.161), channel_id=1, replica_groups=mesh['rep'=2,'ep'=4,'et'=4] {'et'}, use_global_device_ids=true, to_apply=%region_9.10 | all-reduce | flops 256 | bytes 2048 | tf_op jit(solution)/shard_map/psum | solution.py:111
  (53 shorter events, 11.3 us)
Async XLA Ops:
  13.9 26.7 %all-to-all-start = ((bf16[4,1,72]{2,1,0:T(2,128)(2,1)}), bf16[4,1,72]{2,1,0:T(2,128)(2,1)S(1)}, u32[]{:S(2)}, u32[]{:S(2)}) async-start(bf16[4,1,72]{2,1,0:T(2,128)(2,1)} %copy.52), calls=%async_computation | async-start | bytes 4096 | tf_op jit(solution)/shard_map/all_to_all | solution.py:63
  40.6 3.7 %copy-start.3 = (s32[128,2]{0,1:T(2,128)S(1)}, s32[128,2]{0,1:T(2,128)}, u32[]{:S(2)}) copy-start(s32[128,2]{0,1:T(2,128)} %param.9) | copy-start | bytes 3076
  40.6 4.0 %copy-start.2 = (bf16[128,768]{1,0:T(8,128)(2,1)S(1)}, bf16[128,768]{1,0:T(8,128)(2,1)}, u32[]{:S(2)}) copy-start(bf16[128,768]{1,0:T(8,128)(2,1)} %param.8) | copy-start | bytes 589828
  40.7 25.9 %all-to-all-start.2 = ((bf16[4,72,3072]{2,1,0:T(8,128)(2,1)}), bf16[4,72,3072]{2,1,0:T(8,128)(2,1)S(1)}, u32[]{:S(2)}, u32[]{:S(2)}) async-start(bf16[4,72,3072]{2,1,0:T(8,128)(2,1)} %bitcast.10), calls=%async_computation.2 | async-start | bytes 3538944 | tf_op jit(solution)/shard_map/all_to_all | solution.py:57
  66.5 12.0 %copy-start = (bf16[4,72,3072]{2,1,0:T(8,128)(2,1)}, bf16[4,72,3072]{2,1,0:T(8,128)(2,1)S(1)}, u32[]{:S(2)}) copy-start(bf16[4,72,3072]{2,1,0:T(8,128)(2,1)S(1)} %all-to-all-done.2) | copy-start | bytes 5308420
  66.5 25.7 %all-to-all-start.1 = ((bf16[4,72,3072]{2,1,0:T(8,128)(2,1)}), bf16[4,72,3072]{2,1,0:T(8,128)(2,1)S(1)}, u32[]{:S(2)}, u32[]{:S(2)}) async-start(bf16[4,72,3072]{2,1,0:T(8,128)(2,1)} %bitcast.8), calls=%async_computation.1 | async-start | bytes 3538944 | tf_op jit(solution)/shard_map/all_to_all | solution.py:60
  103.0 7.8 %copy-start.5 = (bf16[288,2048]{1,0:T(8,128)(2,1)}, bf16[288,2048]{1,0:T(8,128)(2,1)S(1)}, u32[]{:S(2)}) copy-start(bf16[288,2048]{1,0:T(8,128)(2,1)S(1)} %get-tuple-element.31) | copy-start | bytes 3538948
  103.0 7.8 %copy-start.4 = (bf16[288,2048]{1,0:T(8,128)(2,1)}, bf16[288,2048]{1,0:T(8,128)(2,1)S(1)}, u32[]{:S(2)}) copy-start(bf16[288,2048]{1,0:T(8,128)(2,1)S(1)} %get-tuple-element.32) | copy-start | bytes 3538948
  125.0 26.6 %all-to-all-start.3 = ((bf16[4,72,3072]{2,1,0:T(8,128)(2,1)}), bf16[4,72,3072]{2,1,0:T(8,128)(2,1)}, u32[]{:S(2)}, u32[]{:S(2)}) async-start(bf16[4,72,3072]{2,1,0:T(8,128)(2,1)} %bitcast.12), calls=%async_computation.3 | async-start | bytes 3538944 | tf_op jit(solution)/shard_map/all_to_all | solution.py:100
  129.4 82.7 %reduce-scatter.2.cloned.1.call-start = ((), (), s32[]{:S(2)}) async-start(), calls=%async_computation.6 | async-start | bytes 983040 | tf_op jit(solution)/shard_map/reduce_scatter | solution.py:108
  165.8 15.5 %copy-start.1 = (bf16[4,72,3072]{2,1,0:T(8,128)(2,1)S(1)}, bf16[4,72,3072]{2,1,0:T(8,128)(2,1)}, u32[]{:S(2)}) copy-start(bf16[4,72,3072]{2,1,0:T(8,128)(2,1)} %copy-done) | copy-start | bytes 5308420
  165.8 15.5 %copy-start.6 = (bf16[288,2048]{1,0:T(8,128)(2,1)S(1)}, bf16[288,2048]{1,0:T(8,128)(2,1)}, u32[]{:S(2)}) copy-start(bf16[288,2048]{1,0:T(8,128)(2,1)} %copy-done.5) | copy-start | bytes 3538948
  178.1 12.9 %all-to-all-start.4 = ((bf16[4,1,72]{2,1,0:T(2,128)(2,1)}), bf16[4,1,72]{2,1,0:T(2,128)(2,1)S(1)}, u32[]{:S(2)}, u32[]{:S(2)}) async-start(bf16[4,1,72]{2,1,0:T(2,128)(2,1)} %convert_element_type.101), calls=%async_computation.5 | async-start | bytes 4096 | tf_op jit(solution)/shard_map/all_to_all | solution.py:103
Sparse Core Ops, SparseCore 0:
  165.9 21.9 reduce-scatter.1
where the time goes:
time: 220 us; the launch traced here: 219 us
  matrix products  86.8 us (39%)
  blocking collectives  56.8 us (26%)
  starting transfers between devices  19.3 us (9%)
  waiting for transfers between devices  16.8 us (8%)
  local copies, waits for them, and re-layouts  15.1 us (7%)
  between operations  14.2 us (6%)
  other arithmetic  9.81 us (4%)
    all_gather x1, blocking collectives, body(): lax.all_gather(tokens, 'et', axis=1, tiled=True)  20.5 us
    psum x1, blocking collectives, body(): route_grad = lax.psum(route_sum, 'et')  18.2 us
    all_gather x1, blocking collectives, body(): lax.all_gather(out_grad, 'et', axis=1, tiled=True)  18.1 us
    dot_general x1, matrix products, body(): lax.dot_general(up_delta, w_up, contract_hidden, preferred_element_type=j...  14.2 us
    dot_general x1, matrix products, body(): lax.dot_general(scaled, flat_dy, contract_rows, preferred_element_type=jn...  12.6 us
    dot_general x1, matrix products, body(): lax.dot_general(flat_x, up_delta, contract_rows, preferred_element_type=j...  11.6 us
    dot_general x1, matrix products, body(): lax.dot_general(flat_dy, w_down, contract_hidden, preferred_element_type=...  10.8 us
    dot_general x1, matrix products, body(): lax.dot_general(flat_x, gate_delta, contract_rows, preferred_element_type...  9.72 us
  transfers between devices with their start and end apart: 6, of which 3 were waited for; matrix products, arithmetic and copies ran while one was open for 27% of the time, Pallas kernels for 0%

commit v1 on v0

v1 whole, which is shorter than its diff:
```python
import functools

import jax
import jax.numpy as jnp
from jax import lax
from jax.experimental import pallas as pl
from jax.experimental.pallas import tpu as pltpu
from jax.sharding import PartitionSpec as P

EXP = 4
CAP = 72
MESH = pl.DeviceIdType.MESH
VMEM_LIMIT = 60 * 1024 * 1024


def remote(src, dst, send_sem, recv_sem, device):
    return pltpu.make_async_remote_copy(
        src_ref=src,
        dst_ref=dst,
        send_sem=send_sem,
        recv_sem=recv_sem,
        device_id=device,
        device_id_type=MESH,
    )


def dispatch_kernel(
    n_ep, n_et, tok_ref, dy_ref, ids_ref, w_ref, x_ref, d_ref, sel_ref, scale_ref,
    rows, meta, recv_sem, z_sem, x_sem, s_sem, meta_send, meta_recv,
):
    group = n_ep // EXP
    chips = n_ep // 2
    me, i = lax.axis_index("ep"), lax.axis_index("et")
    chip, core = lax.div(me, 2), lax.rem(me, 2)
    sibling = chip * 2 + 1 - core
    own = (tok_ref, dy_ref)
    width = tok_ref.shape[1]
    count = tok_ref.shape[0]

    barrier = pltpu.get_barrier_semaphore()
    for k in range(1, n_ep):
        pl.semaphore_signal(
            barrier, inc=1, device_id={"ep": lax.rem(me + k, n_ep)}, device_id_type=MESH
        )

    @pl.when(i > 0)
    def _():
        pl.semaphore_signal(barrier, inc=1, device_id={"et": i - 1}, device_id_type=MESH)

    @pl.when(i < n_et - 1)
    def _():
        pl.semaphore_signal(barrier, inc=1, device_id={"et": i + 1}, device_id_type=MESH)

    ids = ids_ref[...]
    weight = w_ref[...]
    experts = lax.broadcasted_iota(jnp.int32, (8, count), 0)
    first, second = ids[0:1, :] == experts, ids[1:2, :] == experts
    hit = jnp.logical_or(first, second)
    earlier = lax.broadcasted_iota(jnp.int32, (count, count), 0) < lax.broadcasted_iota(
        jnp.int32, (count, count), 1
    )
    before = jnp.dot(
        jnp.where(hit, 1.0, 0.0).astype(jnp.bfloat16),
        jnp.where(earlier, 1.0, 0.0).astype(jnp.bfloat16),
        preferred_element_type=jnp.float32,
    )
    meta[me, 0:8, :] = jnp.where(hit, before, -1e6)
    meta[me, 8:16, :] = jnp.where(first, weight[0:1, :], 0.0) + jnp.where(
        second, weight[1:2, :], 0.0
    )

    neighbours = jnp.where(i > 0, 1, 0) + jnp.where(i < n_et - 1, 1, 0)
    pl.semaphore_wait(barrier, n_ep - 1 + neighbours)

    def block(a, p, j):
        return rows.at[a, p, j]

    def z_copy(a, j, way, src):
        return remote(
            src, block(a, me, j), z_sem.at[a, way, j], recv_sem.at[a, me, j],
            {"et": i + 1 if way == 0 else i - 1},
        )

    def x_copy(a, k, j, src):
        peer = lax.rem(chip + k, chips) * 2 + core
        return remote(
            src, block(a, me, j), x_sem.at[a, k, j], recv_sem.at[a, me, j], {"ep": peer}
        )

    def s_copy(a, p, j, src):
        return remote(
            src, block(a, p, j), s_sem.at[a, p, j], recv_sem.at[a, p, j], {"ep": sibling}
        )

    def meta_copy(k):
        return remote(
            meta.at[me], meta.at[me], meta_send.at[k], meta_recv.at[me],
            {"ep": lax.rem(me + k, n_ep)},
        )

    def arrive(a, p, j):
        remote(
            block(a, p, j), block(a, p, j), s_sem.at[a, p, j], recv_sem.at[a, p, j],
            {"ep": sibling},
        ).wait_recv()

    def fan(a, j, src):
        for k in range(1, chips):
            x_copy(a, k, j, src).start()
        s_copy(a, me, j, src).start()

    for k in range(1, n_ep):
        meta_copy(k).start()
    for a in range(2):
        @pl.when(i < n_et - 1)
        def _():
            z_copy(a, i, 0, own[a]).start()

        @pl.when(i > 0)
        def _():
            z_copy(a, i, 1, own[a]).start()

        fan(a, i, own[a])
    for a in range(2):
        rows[a, me, i] = own[a][...]

    def on_steps(s, act):
        @pl.when(i >= s)
        def _():
            act(i - s, 0)

        if s > 0:
            @pl.when(i + s < n_et)
            def _():
                act(i + s, 1)

    def from_chips(s):
        for a in range(2):
            def act(j, way):
                for k in range(1, chips):
                    p = lax.rem(chip + k, chips) * 2 + core
                    arrive(a, p, j)
                    s_copy(a, p, j, block(a, p, j)).start()

            on_steps(s, act)

    for s in range(1, n_et):
        for a in range(2):
            def act(j, way):
                arrive(a, me, j)
                if way == 0:
                    @pl.when(i < n_et - 1)
                    def _():
                        z_copy(a, j, 0, block(a, me, j)).start()
                else:
                    @pl.when(i > 0)
                    def _():
                        z_copy(a, j, 1, block(a, me, j)).start()

                fan(a, j, block(a, me, j))

            on_steps(s, act)
        from_chips(s - 1)
    from_chips(n_et - 1)

    for k in range(1, n_ep):
        p = lax.rem(me + k, n_ep)
        remote(
            meta.at[p], meta.at[p], meta_send.at[k], meta_recv.at[p], {"ep": p}
        ).wait_recv()
    expert = lax.div(me, group)
    slots = n_ep * CAP
    slot_row = lax.broadcasted_iota(jnp.int32, (slots, count), 0).astype(jnp.float32)
    scale = jnp.zeros((slots, 1), jnp.float32)
    for p in range(n_ep):
        place = meta[p, pl.ds(expert, 1), :]
        token_weight = meta[p, pl.ds(expert + 8, 1), :]
        match = slot_row == place + float(p * CAP)
        sel_ref[:, p * count : (p + 1) * count] = jnp.where(match, 1.0, 0.0).astype(jnp.bfloat16)
        scale = scale + jnp.sum(jnp.where(match, token_weight, 0.0), axis=1, keepdims=True)
    scale_ref[...] = jnp.broadcast_to(scale, scale_ref.shape)

    for a, out in ((0, x_ref), (1, d_ref)):
        for q in range(chips):
            for j in range(n_et):
                arrive(a, q * 2 + 1 - core, j)

        @pl.loop(0, n_et)
        def _(j):
            source = rows[a, :, j].reshape(n_ep * count, width)
            out[:, pl.ds(pl.multiple_of(j * width, width), width)] = jnp.dot(
                sel_ref[...], source, preferred_element_type=jnp.float32
            ).astype(jnp.bfloat16)

    for k in range(1, n_ep):
        meta_copy(k).wait_send()
    for a in range(2):
        for j in range(n_et):
            for k in range(1, chips):
                x_copy(a, k, j, block(a, me, j)).wait_send()
            for q in range(chips):
                p = q * 2 + core
                s_copy(a, p, j, block(a, p, j)).wait_send()

            @pl.when(jnp.logical_and(i < n_et - 1, i >= j))
            def _():
                z_copy(a, j, 0, block(a, me, j)).wait_send()

            @pl.when(jnp.logical_and(i > 0, i <= j))
            def _():
                z_copy(a, j, 1, block(a, me, j)).wait_send()


def combine_kernel(
    n_ep, n_et, gd_ref, ud_ref, wg_ref, wu_ref, place_ref, route_ref, ids_ref, tok_ref, rg_ref,
    wg, wu, part, sib_in, total, x_in, z_out, z_in, r_out, r_in, rz_out, rz_in,
    w_sem, s_send, s_recv, x_send, x_recv, z_send, z_recv, r_send, r_recv, rz_send, rz_recv,
):
    group = n_ep // EXP
    chips = n_ep // 2
    me, i = lax.axis_index("ep"), lax.axis_index("et")
    chip, core = lax.div(me, 2), lax.rem(me, 2)
    sibling = chip * 2 + 1 - core
    count, width = tok_ref.shape
    barrier = pltpu.get_barrier_semaphore()
    for k in range(1, n_ep):
        pl.semaphore_signal(
            barrier, inc=1, device_id={"ep": lax.rem(me + k, n_ep)}, device_id_type=MESH
        )
    for k in range(1, n_et):
        pl.semaphore_signal(
            barrier, inc=1, device_id={"et": lax.rem(i + k, n_et)}, device_id_type=MESH
        )

    def owner(s):
        return lax.rem(i + 1 + s, n_et)

    def weights(s):
        at = pl.ds(pl.multiple_of(owner(s) * width, width), width)
        return (
            pltpu.make_async_copy(wg_ref.at[at, :], wg.at[s], w_sem.at[0, s]),
            pltpu.make_async_copy(wu_ref.at[at, :], wu.at[s], w_sem.at[1, s]),
        )

    for s in range(n_et):
        for copy in weights(s):
            copy.start()
    transposed = (((1,), (1,)), ((), ()))
    routes = lax.dot_general(
        route_ref[...], place_ref[...], transposed, preferred_element_type=jnp.float32
    )
    for p in range(n_ep):
        r_out[p] = routes[:, p * count : (p + 1) * count]
    pl.semaphore_wait(barrier, n_ep - 1 + n_et - 1)

    def r_copy(k):
        p = lax.rem(me + k, n_ep)
        return remote(r_out.at[p], r_in.at[me], r_send.at[k], r_recv.at[me], {"ep": p})

    def rz_copy(k):
        return remote(
            rz_out, rz_in.at[i], rz_send.at[k], rz_recv.at[i], {"et": lax.rem(i + k, n_et)}
        )

    def s_copy(s, q):
        return remote(
            part.at[s, q * 2 + 1 - core], sib_in.at[s, q], s_send.at[s, q], s_recv.at[s, q],
            {"ep": sibling},
        )

    def x_copy(s, k):
        q = lax.rem(chip + k, chips)
        return remote(
            total.at[s, q], x_in.at[s, chip], x_send.at[s, k], x_recv.at[s, chip],
            {"ep": q * 2 + core},
        )

    def z_copy(s):
        return remote(
            z_out.at[s], z_in.at[i], z_send.at[s], z_recv.at[i], {"et": owner(s)}
        )

    for k in range(1, n_ep):
        r_copy(k).start()
    r_in[me] = r_out[me]

    def to_chips(s):
        for q in range(chips):
            s_copy(s, q).wait_recv()
            total[s, q] = (
                part[s, q * 2 + core].astype(jnp.float32) + sib_in[s, q].astype(jnp.float32)
            ).astype(jnp.bfloat16)
        for k in range(1, chips):
            x_copy(s, k).start()

    def step(s):
        for copy in weights(s):
            copy.wait()
        piece = lax.dot_general(
            gd_ref[...], wg[s], transposed, preferred_element_type=jnp.float32
        ) + lax.dot_general(ud_ref[...], wu[s], transposed, preferred_element_type=jnp.float32)
        placed = jnp.dot(
            place_ref[...], piece.astype(jnp.bfloat16), preferred_element_type=jnp.float32
        ).astype(jnp.bfloat16)
        part[s] = placed.reshape(n_ep, count, width)
        for q in range(chips):
            s_copy(s, q).start()

    step(0)

    @pl.loop(1, n_et)
    def _(s):
        step(s)
        to_chips(s - 1)

    to_chips(n_et - 1)

    for k in range(1, n_ep):
        p = lax.rem(me + k, n_ep)
        remote(r_out.at[p], r_in.at[p], r_send.at[k], r_recv.at[p], {"ep": p}).wait_recv()
    ids = ids_ref[...]
    route = jnp.zeros(ids.shape, jnp.float32)
    for p in range(n_ep):
        route = route + jnp.where(ids == p // group, r_in[p, 0:1, :], 0.0)
    rz_out[0:2, :] = route
    rz_out[2:8, :] = jnp.zeros((6, count), jnp.float32)
    for k in range(1, n_et):
        rz_copy(k).start()
    rz_in[i] = rz_out[...]

    for s in range(n_et):
        value = total[s, chip].astype(jnp.float32)
        for k in range(1, chips):
            q = lax.rem(chip + k, chips)
            remote(
                total.at[s, q], x_in.at[s, q], x_send.at[s, k], x_recv.at[s, q],
                {"ep": q * 2 + core},
            ).wait_recv()
            value = value + x_in[s, q].astype(jnp.float32)
        if s < n_et - 1:
            z_out[s] = value.astype(jnp.bfloat16)
            z_copy(s).start()
        else:
            z_in[i] = value.astype(jnp.bfloat16)

    for k in range(1, n_et):
        j = lax.rem(i + k, n_et)
        remote(z_in.at[j], z_in.at[j], z_send.at[0], z_recv.at[j], {"et": j}).wait_recv()
        remote(rz_in.at[j], rz_in.at[j], rz_send.at[k], rz_recv.at[j], {"et": j}).wait_recv()
    result = z_in[0].astype(jnp.float32)
    route = rz_in[0]
    for j in range(1, n_et):
        result = result + z_in[j].astype(jnp.float32)
        route = route + rz_in[j]
    tok_ref[...] = result.astype(jnp.bfloat16)
    rg_ref[...] = route

    for k in range(1, n_ep):
        r_copy(k).wait_send()
    for k in range(1, n_et):
        rz_copy(k).wait_send()
    for s in range(n_et):
        for q in range(chips):
            s_copy(s, q).wait_send()
        for k in range(1, chips):
            x_copy(s, k).wait_send()
        if s < n_et - 1:
            z_copy(s).wait_send()


def dispatch(tokens, out_grad, ids, weight, n_ep, n_et):
    count, width = tokens.shape
    slots = n_ep * CAP
    dma = pltpu.SemaphoreType.DMA
    whole = pl.BlockSpec(memory_space=pltpu.VMEM)
    return pl.pallas_call(
        functools.partial(dispatch_kernel, n_ep, n_et),
        out_shape=(
            jax.ShapeDtypeStruct((slots, n_et * width), jnp.bfloat16),
            jax.ShapeDtypeStruct((slots, n_et * width), jnp.bfloat16),
            jax.ShapeDtypeStruct((slots, n_ep * count), jnp.bfloat16),
            jax.ShapeDtypeStruct((slots, 128), jnp.float32),
        ),
        in_specs=[whole] * 4,
        out_specs=(whole,) * 4,
        scratch_shapes=[
            pltpu.VMEM((2, n_ep, n_et, count, width), jnp.bfloat16),
            pltpu.VMEM((n_ep, 16, count), jnp.float32),
            dma((2, n_ep, n_et)),
            dma((2, 2, n_et)),
            dma((2, n_ep // 2, n_et)),
            dma((2, n_ep, n_et)),
            dma((n_ep,)),
            dma((n_ep,)),
        ],
        compiler_params=pltpu.CompilerParams(
            collective_id=0, has_side_effects=True, vmem_limit_bytes=VMEM_LIMIT
        ),
        name="dispatch",
    )(tokens, out_grad, ids, weight)


def combine(gate_delta, up_delta, w_gate, w_up, place, route, ids, count, n_ep, n_et):
    width = w_gate.shape[0] // n_et
    hidden = w_gate.shape[1]
    chips = n_ep // 2
    dma = pltpu.SemaphoreType.DMA
    whole = pl.BlockSpec(memory_space=pltpu.VMEM)
    hbm = pl.BlockSpec(memory_space=pl.ANY)
    bf16, f32 = jnp.bfloat16, jnp.float32
    return pl.pallas_call(
        functools.partial(combine_kernel, n_ep, n_et),
        out_shape=(
            jax.ShapeDtypeStruct((count, width), bf16),
            jax.ShapeDtypeStruct((8, count), f32),
        ),
        in_specs=[whole, whole, hbm, hbm, whole, whole, whole],
        out_specs=(whole, whole),
        scratch_shapes=[
            pltpu.VMEM((n_et, width, hidden), bf16),
            pltpu.VMEM((n_et, width, hidden), bf16),
            pltpu.VMEM((n_et, n_ep, count, width), bf16),
            pltpu.VMEM((n_et, chips, count, width), bf16),
            pltpu.VMEM((n_et, chips, count, width), bf16),
            pltpu.VMEM((n_et, chips, count, width), bf16),
            pltpu.VMEM((n_et, count, width), bf16),
            pltpu.VMEM((n_et, count, width), bf16),
            pltpu.VMEM((n_ep, 8, count), f32),
            pltpu.VMEM((n_ep, 8, count), f32),
            pltpu.VMEM((8, count), f32),
            pltpu.VMEM((n_et, 8, count), f32),
            dma((2, n_et)),
            dma((n_et, chips)),
            dma((n_et, chips)),
            dma((n_et, chips)),
            dma((n_et, chips)),
            dma((n_et,)),
            dma((n_et,)),
            dma((n_ep,)),
            dma((n_ep,)),
            dma((n_et,)),
            dma((n_et,)),
        ],
        compiler_params=pltpu.CompilerParams(
            collective_id=1, has_side_effects=True, vmem_limit_bytes=VMEM_LIMIT
        ),
        name="combine",
    )(gate_delta, up_delta, w_gate, w_up, place, route, ids)


def body(tokens, out_grad, route_ids, route_weight, w_gate, w_up, w_down):
    n_ep, n_et = lax.axis_size("ep"), lax.axis_size("et")
    count = tokens.shape[0]
    ids = route_ids.T
    flat_x, flat_dy, select, scale_wide = dispatch(
        tokens, out_grad, ids, route_weight.T.astype(jnp.float32), n_ep, n_et
    )
    scale = scale_wide[:, 0:1]
    contract_rows = (((0,), (0,)), ((), ()))
    contract_hidden = (((1,), (1,)), ((), ()))
    gate = jnp.dot(flat_x, w_gate, preferred_element_type=jnp.float32)
    upper = jnp.dot(flat_x, w_up, preferred_element_type=jnp.float32)
    sigma = jax.nn.sigmoid(gate)
    silu_gate = gate * sigma
    active = silu_gate * upper
    scaled = (scale * active).astype(jnp.bfloat16)
    raw_grad = lax.dot_general(flat_dy, w_down, contract_hidden, preferred_element_type=jnp.float32)
    slot_route = jnp.sum(active * raw_grad, axis=1).astype(jnp.bfloat16)
    hidden_grad = scale * raw_grad
    gate_delta = (hidden_grad * upper * sigma * (1.0 + gate * (1.0 - sigma))).astype(jnp.bfloat16)
    up_delta = (hidden_grad * silu_gate).astype(jnp.bfloat16)
    route = jnp.broadcast_to(slot_route[None, :], (16, slot_route.shape[0]))[0:8]
    token_grad, route_rows = combine(
        gate_delta, up_delta, w_gate, w_up, select.T, route, ids, count, n_ep, n_et
    )
    gate_grad = lax.dot_general(
        flat_x, gate_delta, contract_rows, preferred_element_type=jnp.float32
    ).astype(jnp.bfloat16)
    up_grad = lax.dot_general(
        flat_x, up_delta, contract_rows, preferred_element_type=jnp.float32
    ).astype(jnp.bfloat16)
    down_grad = lax.dot_general(
        scaled, flat_dy, contract_rows, preferred_element_type=jnp.float32
    ).astype(jnp.bfloat16)
    return (token_grad, route_rows[0:2].T, gate_grad, up_grad, down_grad)


def solution(mesh):
    return jax.shard_map(
        body,
        mesh=mesh,
        in_specs=(
            P(("rep", "ep"), "et"),
            P(("rep", "ep"), "et"),
            P(("rep", "ep"), None),
            P(("rep", "ep"), None),
            P(None, ("ep", "et")),
            P(None, ("ep", "et")),
            P(("ep", "et"), None),
        ),
        out_specs=(
            P(("rep", "ep"), "et"),
            P(("rep", "ep"), None),
            P("rep", ("ep", "et")),
            P("rep", ("ep", "et")),
            P(("ep", "et"), "rep"),
        ),
        check_vma=False,
    )
```

time: 220 us -> 154 us (0.70)
  Pallas kernels: 0 us -> 82.9 us
  blocking collectives: 56.8 us -> 0 us
  matrix products: 86.8 us -> 61.6 us
  starting transfers between devices: 19.3 us -> 0 us
  waiting for transfers between devices: 16.8 us -> 0 us
  between operations: 14.2 us -> 0.69 us
  local copies, waits for them, and re-layouts: 15.1 us -> 5.48 us
  other arithmetic: 9.81 us -> 1.22 us
    pallas_call x0 -> x2, Pallas kernels: none -> 82.9 us  [the longest x1 46.3 us: dispatch(): pl.pallas_call(functools.partial(dispatch_kernel, n_ep, n_et), out_shape=...]
    all_gather x2 -> x0, blocking collectives: 38.6 us -> none  [the longest x1 20.5 us: body(): lax.all_gather(tokens, 'et', axis=1, tiled=True)]
    dot_general x4 -> x0, matrix products: 25.5 us -> none  [the longest x1 14.2 us: body(): lax.dot_general(up_delta, w_up, contract_hidden, preferred_element_type=j...]
    all_to_all x5 -> x0, starting transfers between devices: 19.3 us -> none  [the longest x1 4.39 us: body(): lax.all_to_all(token_half.reshape(senders, CAP, width), 'ep', split_axis=...]
    psum x1 -> x0, blocking collectives: 18.2 us -> none  [body(): route_grad = lax.psum(route_sum, 'et')]
    all_to_all x5 -> x0, waiting for transfers between devices: 16.8 us -> none  [the longest x1 9.55 us: body(): lax.all_to_all(token_half.reshape(senders, CAP, width), 'ep', split_axis=...]
    gather x7 -> x0, local copies, waits for them, and re-layouts: 12.4 us -> none  [the longest x2 7.06 us: unpack_slots(): token_sum = jnp.sum(per_expert[slot_of], axis=1)]
    reduce_sum x4 -> x0, other arithmetic: 6.03 us -> none  [the longest x1 5.17 us: unpack_slots(): token_sum = jnp.sum(per_expert[slot_of], axis=1)]
  transfers between devices with their start and end apart: 6 -> 0, of which waited for: 3 -> 0; matrix products, arithmetic and copies ran while one was open for 27% -> 0% of each run, Pallas kernels for 0% -> 0%
where the time goes in v1:
time: 154 us; the launch traced here: 152 us
  Pallas kernels  82.9 us (54%)
  matrix products  61.6 us (40%)
  local copies, waits for them, and re-layouts  5.48 us (4%)
    pallas_call x1, Pallas kernels, dispatch(): pl.pallas_call(functools.partial(dispatch_kernel, n_ep, n_et), out_shape=...  46.3 us
    pallas_call x1, Pallas kernels, combine(): pl.pallas_call(functools.partial(combine_kernel, n_ep, n_et), out_shape=(...  36.6 us
    dot_general x1, matrix products, body(): lax.dot_general(scaled, flat_dy, contract_rows, preferred_element_type=jn...  12.7 us
    dot_general x1, matrix products, body(): lax.dot_general(flat_dy, w_down, contract_hidden, preferred_element_type=...  11.4 us
    dot_general x1, matrix products, body(): lax.dot_general(flat_x, gate_delta, contract_rows, preferred_element_type...  9.7 us
    dot_general x1, matrix products, body(): lax.dot_general(flat_x, up_delta, contract_rows, preferred_element_type=j...  9.69 us
    dot_general x1, matrix products, body(): upper = jnp.dot(flat_x, w_up, preferred_element_type=jnp.float32)  9.16 us
    dot_general x1, matrix products, body(): gate = jnp.dot(flat_x, w_gate, preferred_element_type=jnp.float32)  8.94 us

profile of v1, /device:TPU:0, one launch (start us, length us, event | category | flops | bytes accessed | tf_op | source)
XLA Modules:
  0.0 151.9 jit_solution(15292548686262037316)
XLA Ops:
  0.6 1.2 convert_bitcast_fusion.w_ref
  1.9 46.3 %dispatch.1 = (bf16[288,3072]{1,0:T(8,128)(2,1)}, bf16[288,3072]{1,0:T(8,128)(2,1)}, bf16[288,512]{1,0:T(8,128)(2,1)}, f32[288,128]{1,0:T(8,128)}) custom-call(bf16[128,768]{1,0:T(8,128)(2,1)} %tok_ref.1, bf16[128,768]{1,0:T(8,128)(2,1)} %dy_ref.1, s32[2,128]{1,0:T(2,128)} %bitcast.18, f32[2,128]{1,0:T(2,128)} %convert_bitcast_fusion.w_ref), custom_call_target="tpu_custom_call" | custom-call | tf_op jit(solution)/shard_map/dispatch/pallas_call | solution.py:376
  48.2 1.1 slice_reduce_fusion
  49.3 1.9 %copy.13 = bf16[288,512]{0,1:T(8,128)(2,1)} copy(bf16[288,512]{1,0:T(8,128)(2,1)} %get-tuple-element.14) | data formatting | bytes 589824 | tf_op jit(solution)/shard_map/dispatch/pallas_call | solution.py:376
  51.1 0.0 copy-start.3
  51.1 8.9 %fusion.5 = f32[288,2048]{1,0:T(8,128)S(1)} fusion(bf16[288,3072]{1,0:T(8,128)(2,1)} %get-tuple-element.13, bf16[3072,2048]{1,0:T(8,128)(2,1)} %wg_ref.1), kind=kOutput, calls=%fused_computation.15 | convolution fusion | flops 3623878656 | bytes 16711680 | tf_op jit(solution)/shard_map/dot_general | solution.py:461
  60.1 0.0 copy-done.3
  60.1 0.0 copy-start.5
  60.1 0.0 copy-start.4
  60.1 9.2 %fusion.4 = f32[288,2048]{1,0:T(8,128)} fusion(bf16[288,3072]{1,0:T(8,128)(2,1)S(1)} %copy-done.3, bf16[3072,2048]{1,0:T(8,128)(2,1)} %wu_ref.1), kind=kOutput, calls=%fused_computation.14 | convolution fusion | flops 3623878656 | bytes 16711680 | tf_op jit(solution)/shard_map/dot_general | solution.py:462
  69.3 0.0 copy-done.5
  69.3 0.0 copy-done.4
  69.3 11.4 %multiply_reduce_fusion = (bf16[288]{0:T(512)(128)(2,1)S(1)}, bf16[288,2048]{1,0:T(8,128)(2,1)}, bf16[288,2048]{1,0:T(8,128)(2,1)}) fusion(f32[288,2048]{1,0:T(8,128)} %fusion.4, f32[288,2048]{1,0:T(8,128)S(1)} %fusion.5, f32[288]{0:T(512)S(1)} %slice_reduce_fusion, bf16[288,3072]{1,0:T(8,128)(2,1)S(1)} %copy-done.4, bf16[2048,3072]{1,0:T(8,128)(2,1)} %param.13), kind=kOutput, calls=%fused_computation.4 | convolution fusion | flops 3633905408 | bytes 21432000 | tf_op jit(solution)/shard_map/dot_general | solution.py:467
  80.7 0.6 slice.10.route_ref
  81.3 36.6 %combine.1 = (bf16[128,768]{1,0:T(8,128)(2,1)}, f32[8,128]{1,0:T(8,128)}) custom-call(bf16[288,2048]{1,0:T(8,128)(2,1)} %get-tuple-element.18.gd_ref, bf16[288,2048]{1,0:T(8,128)(2,1)} %get-tuple-element.19.ud_ref, bf16[3072,2048]{1,0:T(8,128)(2,1)} %wg_ref.1, bf16[3072,2048]{1,0:T(8,128)(2,1)} %wu_ref.1, bf16[512,288]{1,0:T(8,128)(2,1)} %bitcast.17, ...), custom_call_target="tpu_custom_call" | custom-call | tf_op jit(solution)/shard_map/combine/pallas_call | solution.py:411
  117.9 1.2 slice_bitcast_fusion
  119.1 12.7 %convolution_convert_fusion = bf16[2048,3072]{1,0:T(8,128)(2,1)} fusion(bf16[288,3072]{1,0:T(8,128)(2,1)S(1)} %copy-done.4, f32[288]{0:T(512)S(1)} %slice_reduce_fusion, f32[288,2048]{1,0:T(8,128)} %fusion.4, f32[288,2048]{1,0:T(8,128)} %copy-done.5), kind=kOutput, calls=%fused_computation | convolution fusion | flops 3634298880 | bytes 19072128 | tf_op jit(solution)/shard_map/dot_general | solution.py:482
  131.9 0.0 copy-done.1
  131.9 0.0 copy-start
  131.9 9.7 %convolution_convert_fusion.1 = bf16[3072,2048]{1,0:T(8,128)(2,1)} fusion(bf16[288,3072]{1,0:T(8,128)(2,1)S(1)} %copy-done.3, bf16[288,2048]{1,0:T(8,128)(2,1)S(1)} %copy-done.1), kind=kOutput, calls=%fused_computation.1 | convolution fusion | flops 3630170112 | bytes 15532032 | tf_op jit(solution)/shard_map/dot_general | solution.py:479
  141.6 0.0 copy-done
  141.6 9.7 %convolution_convert_fusion.2 = bf16[3072,2048]{1,0:T(8,128)(2,1)} fusion(bf16[288,3072]{1,0:T(8,128)(2,1)S(1)} %copy-done.3, bf16[288,2048]{1,0:T(8,128)(2,1)S(1)} %copy-done), kind=kOutput, calls=%fused_computation.2 | convolution fusion | flops 3630170112 | bytes 15532032 | tf_op jit(solution)/shard_map/dot_general | solution.py:476
  151.3 0.0 copy-done.2
  151.3 0.7 copy.15
  (2 shorter events, 0.0 us)
Async XLA Ops:
  51.1 9.0 %copy-start.3 = (bf16[288,3072]{1,0:T(8,128)(2,1)S(1)}, bf16[288,3072]{1,0:T(8,128)(2,1)}, u32[]{:S(2)}) copy-start(bf16[288,3072]{1,0:T(8,128)(2,1)} %get-tuple-element.13) | copy-start | bytes 5308420
  60.1 9.2 %copy-start.5 = (f32[288,2048]{1,0:T(8,128)}, f32[288,2048]{1,0:T(8,128)S(1)}, u32[]{:S(2)}) copy-start(f32[288,2048]{1,0:T(8,128)S(1)} %fusion.5) | copy-start | bytes 7077892
  60.1 9.2 %copy-start.4 = (bf16[288,3072]{1,0:T(8,128)(2,1)S(1)}, bf16[288,3072]{1,0:T(8,128)(2,1)}, u32[]{:S(2)}) copy-start(bf16[288,3072]{1,0:T(8,128)(2,1)} %get-tuple-element.12) | copy-start | bytes 5308420
  119.1 12.7 %copy-start.1 = (bf16[288,2048]{1,0:T(8,128)(2,1)S(1)}, bf16[288,2048]{1,0:T(8,128)(2,1)}, u32[]{:S(2)}) copy-start(bf16[288,2048]{1,0:T(8,128)(2,1)} %get-tuple-element.19.ud_ref) | copy-start | bytes 3538948
  131.9 9.7 %copy-start = (bf16[288,2048]{1,0:T(8,128)(2,1)S(1)}, bf16[288,2048]{1,0:T(8,128)(2,1)}, u32[]{:S(2)}) copy-start(bf16[288,2048]{1,0:T(8,128)(2,1)} %get-tuple-element.18.gd_ref) | copy-start | bytes 3538948
  141.6 9.7 %copy-start.2 = (bf16[128,768]{1,0:T(8,128)(2,1)S(1)}, bf16[128,768]{1,0:T(8,128)(2,1)}, u32[]{:S(2)}) copy-start(bf16[128,768]{1,0:T(8,128)(2,1)} %get-tuple-element.25) | copy-start | bytes 589828

commit v2 on v1

--- a/solution.py
+++ b/solution.py
@@ -10,7 +10,7 @@
 EXP = 4
 CAP = 72
 MESH = pl.DeviceIdType.MESH
-VMEM_LIMIT = 60 * 1024 * 1024
+VMEM_LIMIT = 62 * 1024 * 1024
 
 
 def remote(src, dst, send_sem, recv_sem, device):
@@ -25,8 +25,10 @@
 
 
 def dispatch_kernel(
-    n_ep, n_et, tok_ref, dy_ref, ids_ref, w_ref, x_ref, d_ref, sel_ref, scale_ref,
-    rows, meta, recv_sem, z_sem, x_sem, s_sem, meta_send, meta_recv,
+    n_ep, n_et, tok_ref, dy_ref, ids_ref, w_ref, wg_ref, wu_ref, wd_ref,
+    x_ref, d_ref, gd_ref, ud_ref, scaled_ref, place_ref, route_ref,
+    rows, meta, sel, stats, wg, wu, wd, gate, upper,
+    recv_sem, z_sem, x_sem, s_sem, meta_send, meta_recv, w_sem,
 ):
     group = n_ep // EXP
     chips = n_ep // 2
@@ -36,6 +38,12 @@
     own = (tok_ref, dy_ref)
     width = tok_ref.shape[1]
     count = tok_ref.shape[0]
+    hidden = wg.shape[1]
+    tile = min(512, hidden)
+    weights = [
+        pltpu.make_async_copy(source, target, w_sem.at[k])
+        for k, (source, target) in enumerate(((wg_ref, wg), (wu_ref, wu), (wd_ref, wd)))
+    ]
 
     barrier = pltpu.get_barrier_semaphore()
     for k in range(1, n_ep):
@@ -109,9 +117,7 @@
             x_copy(a, k, j, src).start()
         s_copy(a, me, j, src).start()
 
-    for k in range(1, n_ep):
-        meta_copy(k).start()
-    for a in range(2):
+    def send_own(a):
         @pl.when(i < n_et - 1)
         def _():
             z_copy(a, i, 0, own[a]).start()
@@ -121,8 +127,6 @@
             z_copy(a, i, 1, own[a]).start()
 
         fan(a, i, own[a])
-    for a in range(2):
-        rows[a, me, i] = own[a][...]
 
     def on_steps(s, act):
         @pl.when(i >= s)
@@ -134,34 +138,57 @@
             def _():
                 act(i + s, 1)
 
-    def from_chips(s):
-        for a in range(2):
-            def act(j, way):
-                for k in range(1, chips):
-                    p = lax.rem(chip + k, chips) * 2 + core
-                    arrive(a, p, j)
-                    s_copy(a, p, j, block(a, p, j)).start()
-
-            on_steps(s, act)
-
+    def from_line(a, s):
+        def act(j, way):
+            arrive(a, me, j)
+            if way == 0:
+                @pl.when(i < n_et - 1)
+                def _():
+                    z_copy(a, j, 0, block(a, me, j)).start()
+            else:
+                @pl.when(i > 0)
+                def _():
+                    z_copy(a, j, 1, block(a, me, j)).start()
+
+            fan(a, j, block(a, me, j))
+
+        on_steps(s, act)
+
+    def from_chips(a, s):
+        def act(j, way):
+            for k in range(1, chips):
+                p = lax.rem(chip + k, chips) * 2 + core
+                arrive(a, p, j)
+                s_copy(a, p, j, block(a, p, j)).start()
+
+        on_steps(s, act)
+
+    def pack(a, out):
+        for q in range(chips):
+            for j in range(n_et):
+                arrive(a, q * 2 + 1 - core, j)
+
+        @pl.loop(0, n_et)
+        def _(j):
+            source = rows[a, :, j].reshape(n_ep * count, width)
+            out[:, pl.ds(pl.multiple_of(j * width, width), width)] = jnp.dot(
+                sel[...], source, preferred_element_type=jnp.float32
+            ).astype(jnp.bfloat16)
+
+    send_own(0)
+    for k in range(1, n_ep):
+        meta_copy(k).start()
+    for copy in weights:
+        copy.start()
+    for a in range(2):
+        rows[a, me, i] = own[a][...]
     for s in range(1, n_et):
-        for a in range(2):
-            def act(j, way):
-                arrive(a, me, j)
-                if way == 0:
-                    @pl.when(i < n_et - 1)
-                    def _():
-                        z_copy(a, j, 0, block(a, me, j)).start()
-                else:
-                    @pl.when(i > 0)
-                    def _():
-                        z_copy(a, j, 1, block(a, me, j)).start()
-
-                fan(a, j, block(a, me, j))
-
-            on_steps(s, act)
-        from_chips(s - 1)
-    from_chips(n_et - 1)
+        from_line(0, s)
+        if s == 1:
+            send_own(1)
+        from_chips(0, s - 1)
+    if n_et == 1:
+        send_own(1)
 
     for k in range(1, n_ep):
         p = lax.rem(me + k, n_ep)
@@ -171,26 +198,76 @@
     expert = lax.div(me, group)
     slots = n_ep * CAP
     slot_row = lax.broadcasted_iota(jnp.int32, (slots, count), 0).astype(jnp.float32)
-    scale = jnp.zeros((slots, 1), jnp.float32)
+    slot_column = lax.broadcasted_iota(jnp.int32, (count, slots), 1).astype(jnp.float32)
+    diagonal = lax.broadcasted_iota(jnp.int32, (count, count), 0) == lax.broadcasted_iota(
+        jnp.int32, (count, count), 1
+    )
+    row_scale = jnp.zeros((slots, 1), jnp.float32)
     for p in range(n_ep):
-        place = meta[p, pl.ds(expert, 1), :]
+        at = slice(p * count, (p + 1) * count)
+        slot = meta[p, pl.ds(expert, 1), :]
         token_weight = meta[p, pl.ds(expert + 8, 1), :]
-        match = slot_row == place + float(p * CAP)
-        sel_ref[:, p * count : (p + 1) * count] = jnp.where(match, 1.0, 0.0).astype(jnp.bfloat16)
-        scale = scale + jnp.sum(jnp.where(match, token_weight, 0.0), axis=1, keepdims=True)
-    scale_ref[...] = jnp.broadcast_to(scale, scale_ref.shape)
-
-    for a, out in ((0, x_ref), (1, d_ref)):
-        for q in range(chips):
-            for j in range(n_et):
-                arrive(a, q * 2 + 1 - core, j)
-
-        @pl.loop(0, n_et)
-        def _(j):
-            source = rows[a, :, j].reshape(n_ep * count, width)
-            out[:, pl.ds(pl.multiple_of(j * width, width), width)] = jnp.dot(
-                sel_ref[...], source, preferred_element_type=jnp.float32
-            ).astype(jnp.bfloat16)
+        match = slot_row == slot + float(p * CAP)
+        sel[:, at] = jnp.where(match, 1.0, 0.0).astype(jnp.bfloat16)
+        row_scale = row_scale + jnp.sum(
+            jnp.where(match, token_weight, 0.0), axis=1, keepdims=True
+        )
+        column = jnp.sum(jnp.where(diagonal, slot, 0.0), axis=1, keepdims=True)
+        place_ref[at, :] = jnp.where(
+            slot_column == column + float(p * CAP), 1.0, 0.0
+        ).astype(jnp.bfloat16)
+    right = lax.broadcasted_iota(jnp.int32, stats.shape, 1) >= 64
+    stats[...] = jnp.where(right, 0.0, row_scale)
+
+    if n_et > 1:
+        from_line(1, 1)
+    from_chips(0, n_et - 1)
+    pack(0, x_ref)
+    pending = [functools.partial(from_chips, 1, 0)]
+    for s in range(2, n_et):
+        pending.append(functools.partial(from_line, 1, s))
+        pending.append(functools.partial(from_chips, 1, s - 1))
+    if n_et > 1:
+        pending.append(functools.partial(from_chips, 1, n_et - 1))
+    pending.reverse()
+    weights[0].wait()
+    weights[1].wait()
+    for c in range(hidden // tile):
+        at = slice(c * tile, (c + 1) * tile)
+        for target, matrix in ((gate, wg), (upper, wu)):
+            target[:, at] = jnp.dot(
+                x_ref[...], matrix[:, at], preferred_element_type=jnp.float32
+            )
+            if pending:
+                pending.pop()()
+    while pending:
+        pending.pop()()
+    weights[2].wait()
+    pack(1, d_ref)
+
+    @pl.loop(0, hidden // tile)
+    def _(c):
+        start = pl.multiple_of(c * tile, tile)
+        at = pl.ds(start, tile)
+        raw = lax.dot_general(
+            d_ref[...], wd[at, :], (((1,), (1,)), ((), ())), preferred_element_type=jnp.float32
+        )
+        g, u, weight = gate[:, at], upper[:, at], stats[:, 0:1]
+        sigma = jax.nn.sigmoid(g)
+        silu = g * sigma
+        active = silu * u
+        scaled_ref[:, at] = (weight * active).astype(jnp.bfloat16)
+        stats[...] += jnp.where(right, jnp.sum(active * raw, axis=1, keepdims=True), 0.0)
+        hidden_grad = weight * raw
+        gd_ref[:, at] = (hidden_grad * u * sigma * (1.0 + g * (1.0 - sigma))).astype(jnp.bfloat16)
+        ud_ref[:, at] = (hidden_grad * silu).astype(jnp.bfloat16)
+
+    slot_route = stats[:, 64:65].astype(jnp.bfloat16).astype(jnp.float32)
+    for p in range(n_ep):
+        chosen = sel[:, p * count : (p + 1) * count].astype(jnp.float32)
+        route_ref[p] = jnp.broadcast_to(
+            jnp.sum(chosen * slot_route, axis=0, keepdims=True), (8, count)
+        )
 
     for k in range(1, n_ep):
         meta_copy(k).wait_send()
@@ -212,8 +289,8 @@
 
 
 def combine_kernel(
-    n_ep, n_et, gd_ref, ud_ref, wg_ref, wu_ref, place_ref, route_ref, ids_ref, tok_ref, rg_ref,
-    wg, wu, part, sib_in, total, x_in, z_out, z_in, r_out, r_in, rz_out, rz_in,
+    n_ep, n_et, gd_ref, ud_ref, wg_ref, wu_ref, place_ref, r_out, ids_ref, tok_ref, rg_ref,
+    wg, wu, part, sib_in, total, x_in, z_out, z_in, r_in, rz_out, rz_in,
     w_sem, s_send, s_recv, x_send, x_recv, z_send, z_recv, r_send, r_recv, rz_send, rz_recv,
 ):
     group = n_ep // EXP
@@ -246,11 +323,6 @@
         for copy in weights(s):
             copy.start()
     transposed = (((1,), (1,)), ((), ()))
-    routes = lax.dot_general(
-        route_ref[...], place_ref[...], transposed, preferred_element_type=jnp.float32
-    )
-    for p in range(n_ep):
-        r_out[p] = routes[:, p * count : (p + 1) * count]
     pl.semaphore_wait(barrier, n_ep - 1 + n_et - 1)
 
     def r_copy(k):
@@ -368,36 +440,50 @@
             z_copy(s).wait_send()
 
 
-def dispatch(tokens, out_grad, ids, weight, n_ep, n_et):
+def dispatch(tokens, out_grad, ids, weight, w_gate, w_up, w_down, n_ep, n_et):
     count, width = tokens.shape
     slots = n_ep * CAP
+    hidden = w_gate.shape[1]
     dma = pltpu.SemaphoreType.DMA
+    bf16, f32 = jnp.bfloat16, jnp.float32
     whole = pl.BlockSpec(memory_space=pltpu.VMEM)
+    hbm = pl.BlockSpec(memory_space=pl.ANY)
     return pl.pallas_call(
         functools.partial(dispatch_kernel, n_ep, n_et),
         out_shape=(
-            jax.ShapeDtypeStruct((slots, n_et * width), jnp.bfloat16),
-            jax.ShapeDtypeStruct((slots, n_et * width), jnp.bfloat16),
-            jax.ShapeDtypeStruct((slots, n_ep * count), jnp.bfloat16),
-            jax.ShapeDtypeStruct((slots, 128), jnp.float32),
+            jax.ShapeDtypeStruct((slots, n_et * width), bf16),
+            jax.ShapeDtypeStruct((slots, n_et * width), bf16),
+            jax.ShapeDtypeStruct((slots, hidden), bf16),
+            jax.ShapeDtypeStruct((slots, hidden), bf16),
+            jax.ShapeDtypeStruct((slots, hidden), bf16),
+            jax.ShapeDtypeStruct((n_ep * count, slots), bf16),
+            jax.ShapeDtypeStruct((n_ep, 8, count), f32),
         ),
-        in_specs=[whole] * 4,
-        out_specs=(whole,) * 4,
+        in_specs=[whole] * 4 + [hbm] * 3,
+        out_specs=(whole,) * 7,
         scratch_shapes=[
-            pltpu.VMEM((2, n_ep, n_et, count, width), jnp.bfloat16),
-            pltpu.VMEM((n_ep, 16, count), jnp.float32),
+            pltpu.VMEM((2, n_ep, n_et, count, width), bf16),
+            pltpu.VMEM((n_ep, 16, count), f32),
+            pltpu.VMEM((slots, n_ep * count), bf16),
+            pltpu.VMEM((slots, 128), f32),
+            pltpu.VMEM(w_gate.shape, bf16),
+            pltpu.VMEM(w_up.shape, bf16),
+            pltpu.VMEM(w_down.shape, bf16),
+            pltpu.VMEM((slots, hidden), f32),
+            pltpu.VMEM((slots, hidden), f32),
             dma((2, n_ep, n_et)),
             dma((2, 2, n_et)),
             dma((2, n_ep // 2, n_et)),
             dma((2, n_ep, n_et)),
             dma((n_ep,)),
             dma((n_ep,)),
+            dma((3,)),
         ],
         compiler_params=pltpu.CompilerParams(
             collective_id=0, has_side_effects=True, vmem_limit_bytes=VMEM_LIMIT
         ),
         name="dispatch",
-    )(tokens, out_grad, ids, weight)
+    )(tokens, out_grad, ids, weight, w_gate, w_up, w_down)
 
 
 def combine(gate_delta, up_delta, w_gate, w_up, place, route, ids, count, n_ep, n_et):
@@ -426,7 +512,6 @@
             pltpu.VMEM((n_et, count, width), bf16),
             pltpu.VMEM((n_et, count, width), bf16),
             pltpu.VMEM((n_ep, 8, count), f32),
-            pltpu.VMEM((n_ep, 8, count), f32),
             pltpu.VMEM((8, count), f32),
             pltpu.VMEM((n_et, 8, count), f32),
             dma((2, n_et)),
@@ -452,27 +537,13 @@
     n_ep, n_et = lax.axis_size("ep"), lax.axis_size("et")
     count = tokens.shape[0]
     ids = route_ids.T
-    flat_x, flat_dy, select, scale_wide = dispatch(
-        tokens, out_grad, ids, route_weight.T.astype(jnp.float32), n_ep, n_et
-    )
-    scale = scale_wide[:, 0:1]
+    flat_x, flat_dy, gate_delta, up_delta, scaled, place, route = dispatch(
+        tokens, out_grad, ids, route_weight.T.astype(jnp.float32), w_gate, w_up, w_down, n_ep, n_et
+    )
+    token_grad, route_rows = combine(
+        gate_delta, up_delta, w_gate, w_up, place, route, ids, count, n_ep, n_et
+    )
     contract_rows = (((0,), (0,)), ((), ()))
-    contract_hidden = (((1,), (1,)), ((), ()))
-    gate = jnp.dot(flat_x, w_gate, preferred_element_type=jnp.float32)
-    upper = jnp.dot(flat_x, w_up, preferred_element_type=jnp.float32)
-    sigma = jax.nn.sigmoid(gate)
-    silu_gate = gate * sigma
-    active = silu_gate * upper
-    scaled = (scale * active).astype(jnp.bfloat16)
-    raw_grad = lax.dot_general(flat_dy, w_down, contract_hidden, preferred_element_type=jnp.float32)
-    slot_route = jnp.sum(active * raw_grad, axis=1).astype(jnp.bfloat16)
-    hidden_grad = scale * raw_grad
-    gate_delta = (hidden_grad * upper * sigma * (1.0 + gate * (1.0 - sigma))).astype(jnp.bfloat16)
-    up_delta = (hidden_grad * silu_gate).astype(jnp.bfloat16)
-    route = jnp.broadcast_to(slot_route[None, :], (16, slot_route.shape[0]))[0:8]
-    token_grad, route_rows = combine(
-        gate_delta, up_delta, w_gate, w_up, select.T, route, ids, count, n_ep, n_et
-    )
     gate_grad = lax.dot_general(
         flat_x, gate_delta, contract_rows, preferred_element_type=jnp.float32
     ).astype(jnp.bfloat16)

time: 154 us -> 131 us (0.85)
  matrix products: 61.6 us -> 30.9 us
  Pallas kernels: 82.9 us -> 94.6 us
  local copies, waits for them, and re-layouts: 5.48 us -> 1.94 us
    dot_general x3 -> x0, matrix products: 29.5 us -> none  [the longest x1 11.4 us: body(): lax.dot_general(flat_dy, w_down, contract_hidden, preferred_element_type=...]
    pallas_call x1, Pallas kernels: 46.3 us -> 59.9 us  [dispatch(): pl.pallas_call(functools.partial(dispatch_kernel, n_ep, n_et), out_shape=...]
    dot_general x1, matrix products: 12.7 us -> 9.9 us  [body(): lax.dot_general(scaled, flat_dy, contract_rows, preferred_element_type=jn...]
    pallas_call x1 -> x0, local copies, waits for them, and re-layouts: 1.89 us -> none  [dispatch(): pl.pallas_call(functools.partial(dispatch_kernel, n_ep, n_et), out_shape=...]
    pallas_call x1, Pallas kernels: 36.6 us -> 34.7 us  [combine(): pl.pallas_call(functools.partial(combine_kernel, n_ep, n_et), out_shape=(...]
    slice x2 -> x0, local copies, waits for them, and re-layouts: 1.65 us -> none  [the longest x1 1.05 us: body(): scale = scale_wide[:, 0:1]]
    dot_general x1, matrix products: 9.69 us -> 11.3 us  [body(): lax.dot_general(flat_x, up_delta, contract_rows, preferred_element_type=j...]
where the time goes in v2:
time: 131 us; the launch traced here: 129 us
  Pallas kernels  94.6 us (72%)
  matrix products  30.9 us (24%)
  local copies, waits for them, and re-layouts  1.94 us (1%)
    pallas_call x1, Pallas kernels, dispatch(): pl.pallas_call(functools.partial(dispatch_kernel, n_ep, n_et), out_shape=...  59.9 us
    pallas_call x1, Pallas kernels, combine(): pl.pallas_call(functools.partial(combine_kernel, n_ep, n_et), out_shape=(...  34.7 us
    dot_general x1, matrix products, body(): lax.dot_general(flat_x, up_delta, contract_rows, preferred_element_type=j...  11.3 us
    dot_general x1, matrix products, body(): lax.dot_general(scaled, flat_dy, contract_rows, preferred_element_type=jn...  9.9 us
    dot_general x1, matrix products, body(): lax.dot_general(flat_x, gate_delta, contract_rows, preferred_element_type...  9.7 us

profile of v2, /device:TPU:0, one launch (start us, length us, event | category | flops | bytes accessed | tf_op | source)
XLA Modules:
  0.0 129.4 jit_solution(12632437304311070105)
XLA Ops:
  0.6 1.2 convert_bitcast_fusion.w_ref
  1.9 59.9 %dispatch.1 = (bf16[288,3072]{1,0:T(8,128)(2,1)}, bf16[288,3072]{1,0:T(8,128)(2,1)}, bf16[288,2048]{1,0:T(8,128)(2,1)}, bf16[288,2048]{1,0:T(8,128)(2,1)}, bf16[...) custom-call(bf16[128,768]{1,0:T(8,128)(2,1)} %tok_ref.1, bf16[128,768]{1,0:T(8,128)(2,1)} %dy_ref.1, ...), custom_call_target="tpu_custom_call" | custom-call | tf_op jit(solution)/shard_map/dispatch/pallas_call | solution.py:451
  61.7 0.0 copy-start.1
  61.7 34.7 %combine.1 = (bf16[128,768]{1,0:T(8,128)(2,1)}, f32[8,128]{1,0:T(8,128)}) custom-call(bf16[288,2048]{1,0:T(8,128)(2,1)} %get-tuple-element.14.gd_ref, bf16[288,2048]{1,0:T(8,128)(2,1)} %get-tuple-element.15.ud_ref, bf16[3072,2048]{1,0:T(8,128)(2,1)} %wg_ref.3, bf16[3072,2048]{1,0:T(8,128)(2,1)} %wu_ref.3, bf16[512,288]{1,0:T(8,128)(2,1)} %get-tuple-element.16.place_ref, ...), custom_call_target="tpu_custom_call" | custom-call | tf_op jit(solution)/shard_map/combine/pallas_call | solution.py:497
  96.5 1.2 slice_bitcast_fusion
  97.7 0.0 copy-done.1
  97.7 0.0 copy-start
  97.7 0.0 copy-start.4
  97.7 11.3 %convolution_convert_fusion.1 = bf16[3072,2048]{1,0:T(8,128)(2,1)} fusion(bf16[288,3072]{1,0:T(8,128)(2,1)} %get-tuple-element.20, bf16[288,2048]{1,0:T(8,128)(2,1)S(1)} %copy-done.1), kind=kOutput, calls=%fused_computation.1 | convolution fusion | flops 3630170112 | bytes 15532032 | tf_op jit(solution)/shard_map/dot_general | solution.py:550
  109.0 0.0 copy-done
  109.0 0.0 copy-done.4
  109.0 0.0 copy-start.3
  109.1 0.0 copy-start.5
  109.1 9.7 %convolution_convert_fusion.2 = bf16[3072,2048]{1,0:T(8,128)(2,1)} fusion(bf16[288,3072]{1,0:T(8,128)(2,1)S(1)} %copy-done.4, bf16[288,2048]{1,0:T(8,128)(2,1)S(1)} %copy-done), kind=kOutput, calls=%fused_computation.2 | convolution fusion | flops 3630170112 | bytes 15532032 | tf_op jit(solution)/shard_map/dot_general | solution.py:547
  118.8 0.0 copy-done.3
  118.8 0.0 copy-done.5
  118.8 0.0 copy-start.2
  118.8 9.9 %convolution_convert_fusion = bf16[2048,3072]{1,0:T(8,128)(2,1)} fusion(bf16[288,2048]{1,0:T(8,128)(2,1)S(1)} %copy-done.5, bf16[288,3072]{1,0:T(8,128)(2,1)S(1)} %copy-done.3), kind=kOutput, calls=%fused_computation | convolution fusion | flops 3630170112 | bytes 15532032 | tf_op jit(solution)/shard_map/dot_general | solution.py:553
  128.7 0.0 copy-done.2
  128.7 0.7 copy.13
Async XLA Ops:
  61.7 36.0 %copy-start.1 = (bf16[288,2048]{1,0:T(8,128)(2,1)S(1)}, bf16[288,2048]{1,0:T(8,128)(2,1)}, u32[]{:S(2)}) copy-start(bf16[288,2048]{1,0:T(8,128)(2,1)} %get-tuple-element.15.ud_ref) | copy-start | bytes 3538948
  97.7 11.3 %copy-start = (bf16[288,2048]{1,0:T(8,128)(2,1)S(1)}, bf16[288,2048]{1,0:T(8,128)(2,1)}, u32[]{:S(2)}) copy-start(bf16[288,2048]{1,0:T(8,128)(2,1)} %get-tuple-element.14.gd_ref) | copy-start | bytes 3538948
  97.7 11.3 %copy-start.4 = (bf16[288,3072]{1,0:T(8,128)(2,1)S(1)}, bf16[288,3072]{1,0:T(8,128)(2,1)}, u32[]{:S(2)}) copy-start(bf16[288,3072]{1,0:T(8,128)(2,1)} %get-tuple-element.20) | copy-start | bytes 5308420
  109.0 9.7 %copy-start.3 = (bf16[288,3072]{1,0:T(8,128)(2,1)S(1)}, bf16[288,3072]{1,0:T(8,128)(2,1)}, u32[]{:S(2)}) copy-start(bf16[288,3072]{1,0:T(8,128)(2,1)} %get-tuple-element.22) | copy-start | bytes 5308420
  109.1 9.7 %copy-start.5 = (bf16[288,2048]{1,0:T(8,128)(2,1)S(1)}, bf16[288,2048]{1,0:T(8,128)(2,1)}, u32[]{:S(2)}) copy-start(bf16[288,2048]{1,0:T(8,128)(2,1)} %get-tuple-element.21) | copy-start | bytes 3538948
  118.8 9.9 %copy-start.2 = (bf16[128,768]{1,0:T(8,128)(2,1)S(1)}, bf16[128,768]{1,0:T(8,128)(2,1)}, u32[]{:S(2)}) copy-start(bf16[128,768]{1,0:T(8,128)(2,1)} %get-tuple-element.28) | copy-start | bytes 589828

commit v3 on v2

--- a/solution.py
+++ b/solution.py
@@ -299,6 +299,9 @@
     chip, core = lax.div(me, 2), lax.rem(me, 2)
     sibling = chip * 2 + 1 - core
     count, width = tok_ref.shape
+    sub = wg.shape[1]
+    pieces = width // sub
+    steps = n_et * pieces
     barrier = pltpu.get_barrier_semaphore()
     for k in range(1, n_ep):
         pl.semaphore_signal(
@@ -310,18 +313,21 @@
         )
 
     def owner(s):
-        return lax.rem(i + 1 + s, n_et)
+        return lax.rem(i + 1 + lax.div(s, pieces), n_et)
 
     def weights(s):
-        at = pl.ds(pl.multiple_of(owner(s) * width, width), width)
+        first = owner(s) * width + lax.rem(s, pieces) * sub
+        at = pl.ds(pl.multiple_of(first, sub), sub)
         return (
             pltpu.make_async_copy(wg_ref.at[at, :], wg.at[s], w_sem.at[0, s]),
             pltpu.make_async_copy(wu_ref.at[at, :], wu.at[s], w_sem.at[1, s]),
         )
 
-    for s in range(n_et):
+    @pl.loop(0, steps)
+    def _(s):
         for copy in weights(s):
             copy.start()
+
     transposed = (((1,), (1,)), ((), ()))
     pl.semaphore_wait(barrier, n_ep - 1 + n_et - 1)
 
@@ -349,7 +355,8 @@
 
     def z_copy(s):
         return remote(
-            z_out.at[s], z_in.at[i], z_send.at[s], z_recv.at[i], {"et": owner(s)}
+            z_out.at[s], z_in.at[i, lax.rem(s, pieces)], z_send.at[s],
+            z_recv.at[i, lax.rem(s, pieces)], {"et": owner(s)},
         )
 
     for k in range(1, n_ep):
@@ -374,18 +381,18 @@
         placed = jnp.dot(
             place_ref[...], piece.astype(jnp.bfloat16), preferred_element_type=jnp.float32
         ).astype(jnp.bfloat16)
-        part[s] = placed.reshape(n_ep, count, width)
+        part[s] = placed.reshape(n_ep, count, sub)
         for q in range(chips):
             s_copy(s, q).start()
 
     step(0)
 
-    @pl.loop(1, n_et)
+    @pl.loop(1, steps)
     def _(s):
         step(s)
         to_chips(s - 1)
 
-    to_chips(n_et - 1)
+    to_chips(steps - 1)
 
     for k in range(1, n_ep):
         p = lax.rem(me + k, n_ep)
@@ -400,7 +407,7 @@
         rz_copy(k).start()
     rz_in[i] = rz_out[...]
 
-    for s in range(n_et):
+    def gather_chips(s):
         value = total[s, chip].astype(jnp.float32)
         for k in range(1, chips):
             q = lax.rem(chip + k, chips)
@@ -409,35 +416,48 @@
                 {"ep": q * 2 + core},
             ).wait_recv()
             value = value + x_in[s, q].astype(jnp.float32)
-        if s < n_et - 1:
-            z_out[s] = value.astype(jnp.bfloat16)
-            z_copy(s).start()
-        else:
-            z_in[i] = value.astype(jnp.bfloat16)
+        return value.astype(jnp.bfloat16)
+
+    @pl.loop(0, steps - pieces)
+    def _(s):
+        z_out[s] = gather_chips(s)
+        z_copy(s).start()
+
+    for u in range(pieces):
+        z_in[i, u] = gather_chips(steps - pieces + u)
 
     for k in range(1, n_et):
         j = lax.rem(i + k, n_et)
-        remote(z_in.at[j], z_in.at[j], z_send.at[0], z_recv.at[j], {"et": j}).wait_recv()
+        for u in range(pieces):
+            remote(
+                z_in.at[j, u], z_in.at[j, u], z_send.at[0], z_recv.at[j, u], {"et": j}
+            ).wait_recv()
         remote(rz_in.at[j], rz_in.at[j], rz_send.at[k], rz_recv.at[j], {"et": j}).wait_recv()
-    result = z_in[0].astype(jnp.float32)
     route = rz_in[0]
     for j in range(1, n_et):
-        result = result + z_in[j].astype(jnp.float32)
         route = route + rz_in[j]
-    tok_ref[...] = result.astype(jnp.bfloat16)
+    for u in range(pieces):
+        result = z_in[0, u].astype(jnp.float32)
+        for j in range(1, n_et):
+            result = result + z_in[j, u].astype(jnp.float32)
+        tok_ref[:, u * sub : (u + 1) * sub] = result.astype(jnp.bfloat16)
     rg_ref[...] = route
 
     for k in range(1, n_ep):
         r_copy(k).wait_send()
     for k in range(1, n_et):
         rz_copy(k).wait_send()
-    for s in range(n_et):
+
+    @pl.loop(0, steps)
+    def _(s):
         for q in range(chips):
             s_copy(s, q).wait_send()
         for k in range(1, chips):
             x_copy(s, k).wait_send()
-        if s < n_et - 1:
-            z_copy(s).wait_send()
+
+    @pl.loop(0, steps - pieces)
+    def _(s):
+        z_copy(s).wait_send()
 
 
 def dispatch(tokens, out_grad, ids, weight, w_gate, w_up, w_down, n_ep, n_et):
@@ -490,6 +510,9 @@
     width = w_gate.shape[0] // n_et
     hidden = w_gate.shape[1]
     chips = n_ep // 2
+    sub = 256 if width % 256 == 0 else 128
+    pieces = width // sub
+    steps = n_et * pieces
     dma = pltpu.SemaphoreType.DMA
     whole = pl.BlockSpec(memory_space=pltpu.VMEM)
     hbm = pl.BlockSpec(memory_space=pl.ANY)
@@ -503,24 +526,24 @@
         in_specs=[whole, whole, hbm, hbm, whole, whole, whole],
         out_specs=(whole, whole),
         scratch_shapes=[
-            pltpu.VMEM((n_et, width, hidden), bf16),
-            pltpu.VMEM((n_et, width, hidden), bf16),
-            pltpu.VMEM((n_et, n_ep, count, width), bf16),
-            pltpu.VMEM((n_et, chips, count, width), bf16),
-            pltpu.VMEM((n_et, chips, count, width), bf16),
-            pltpu.VMEM((n_et, chips, count, width), bf16),
-            pltpu.VMEM((n_et, count, width), bf16),
-            pltpu.VMEM((n_et, count, width), bf16),
+            pltpu.VMEM((steps, sub, hidden), bf16),
+            pltpu.VMEM((steps, sub, hidden), bf16),
+            pltpu.VMEM((steps, n_ep, count, sub), bf16),
+            pltpu.VMEM((steps, chips, count, sub), bf16),
+            pltpu.VMEM((steps, chips, count, sub), bf16),
+            pltpu.VMEM((steps, chips, count, sub), bf16),
+            pltpu.VMEM((steps, count, sub), bf16),
+            pltpu.VMEM((n_et, pieces, count, sub), bf16),
             pltpu.VMEM((n_ep, 8, count), f32),
             pltpu.VMEM((8, count), f32),
             pltpu.VMEM((n_et, 8, count), f32),
-            dma((2, n_et)),
-            dma((n_et, chips)),
-            dma((n_et, chips)),
-            dma((n_et, chips)),
-            dma((n_et, chips)),
-            dma((n_et,)),
-            dma((n_et,)),
+            dma((2, steps)),
+            dma((steps, chips)),
+            dma((steps, chips)),
+            dma((steps, chips)),
+            dma((steps, chips)),
+            dma((steps,)),
+            dma((n_et, pieces)),
             dma((n_ep,)),
             dma((n_ep,)),
             dma((n_et,)),
@@ -533,6 +556,46 @@
     )(gate_delta, up_delta, w_gate, w_up, place, route, ids)
 
 
+def grads_kernel(x_ref, gd_ref, ud_ref, scaled_ref, d_ref, gate_ref, up_ref, down_ref):
+    contract_rows = (((0,), (0,)), ((), ()))
+    for left, right, out in (
+        (x_ref, gd_ref, gate_ref), (x_ref, ud_ref, up_ref), (scaled_ref, d_ref, down_ref)
+    ):
+        out[...] = lax.dot_general(
+            left[...], right[...], contract_rows, preferred_element_type=jnp.float32
+        ).astype(jnp.bfloat16)
+
+
+def weight_grads(x, gate_delta, up_delta, scaled, dy):
+    slots, width = x.shape
+    hidden = gate_delta.shape[1]
+    steps = max(1, hidden // 256)
+    rows, hidden_rows = width // steps, hidden // steps
+
+    def full(columns):
+        return pl.BlockSpec((slots, columns), lambda t: (0, 0))
+
+    def columns_of(size):
+        return pl.BlockSpec((slots, size), lambda t: (0, t))
+
+    def rows_of(size, columns):
+        return pl.BlockSpec((size, columns), lambda t: (t, 0))
+
+    return pl.pallas_call(
+        grads_kernel,
+        grid=(steps,),
+        in_specs=[columns_of(rows), full(hidden), full(hidden), columns_of(hidden_rows), full(width)],
+        out_specs=(rows_of(rows, hidden), rows_of(rows, hidden), rows_of(hidden_rows, width)),
+        out_shape=(
+            jax.ShapeDtypeStruct((width, hidden), jnp.bfloat16),
+            jax.ShapeDtypeStruct((width, hidden), jnp.bfloat16),
+            jax.ShapeDtypeStruct((hidden, width), jnp.bfloat16),
+        ),
+        compiler_params=pltpu.CompilerParams(vmem_limit_bytes=VMEM_LIMIT),
+        name="weight_grads",
+    )(x, gate_delta, up_delta, scaled, dy)
+
+
 def body(tokens, out_grad, route_ids, route_weight, w_gate, w_up, w_down):
     n_ep, n_et = lax.axis_size("ep"), lax.axis_size("et")
     count = tokens.shape[0]
@@ -543,16 +606,7 @@
     token_grad, route_rows = combine(
         gate_delta, up_delta, w_gate, w_up, place, route, ids, count, n_ep, n_et
     )
-    contract_rows = (((0,), (0,)), ((), ()))
-    gate_grad = lax.dot_general(
-        flat_x, gate_delta, contract_rows, preferred_element_type=jnp.float32
-    ).astype(jnp.bfloat16)
-    up_grad = lax.dot_general(
-        flat_x, up_delta, contract_rows, preferred_element_type=jnp.float32
-    ).astype(jnp.bfloat16)
-    down_grad = lax.dot_general(
-        scaled, flat_dy, contract_rows, preferred_element_type=jnp.float32
-    ).astype(jnp.bfloat16)
+    gate_grad, up_grad, down_grad = weight_grads(flat_x, gate_delta, up_delta, scaled, flat_dy)
     return (token_grad, route_rows[0:2].T, gate_grad, up_grad, down_grad)
 
 

time: 131 us -> 130 us (level)
  matrix products: 30.9 us -> 0 us
  Pallas kernels: 94.6 us -> 124 us
    dot_general x3 -> x0, matrix products: 30.9 us -> none  [the longest x1 11.3 us: body(): lax.dot_general(flat_x, up_delta, contract_rows, preferred_element_type=j...]
    pallas_call x0 -> x1, Pallas kernels: none -> 24.9 us  [weight_grads(): pl.pallas_call(grads_kernel, grid=(steps,), in_specs=[columns_of(rows), f...]
    pallas_call x1, Pallas kernels: 34.7 us -> 39 us  [combine(): pl.pallas_call(functools.partial(combine_kernel, n_ep, n_et), out_shape=(...]
where the time goes in v3:
time: 130 us; the launch traced here: 128 us
  Pallas kernels  124 us (95%)
  local copies, waits for them, and re-layouts  2.86 us (2%)
    pallas_call x1, Pallas kernels, dispatch(): pl.pallas_call(functools.partial(dispatch_kernel, n_ep, n_et), out_shape=...  59.9 us
    pallas_call x1, Pallas kernels, combine(): pl.pallas_call(functools.partial(combine_kernel, n_ep, n_et), out_shape=(...  39 us
    pallas_call x1, Pallas kernels, weight_grads(): pl.pallas_call(grads_kernel, grid=(steps,), in_specs=[columns_of(rows), f...  24.9 us

profile of v3, /device:TPU:0, one launch (start us, length us, event | category | flops | bytes accessed | tf_op | source)
XLA Modules:
  0.0 128.4 jit_solution(3798901660713149332)
XLA Ops:
  0.6 1.2 convert_bitcast_fusion.w_ref
  1.9 59.9 %dispatch.1 = (bf16[288,3072]{1,0:T(8,128)(2,1)}, bf16[288,3072]{1,0:T(8,128)(2,1)}, bf16[288,2048]{1,0:T(8,128)(2,1)}, bf16[288,2048]{1,0:T(8,128)(2,1)}, bf16[...) custom-call(bf16[128,768]{1,0:T(8,128)(2,1)} %tok_ref.1, bf16[128,768]{1,0:T(8,128)(2,1)} %dy_ref.1, ...), custom_call_target="tpu_custom_call" | custom-call | tf_op jit(solution)/shard_map/dispatch/pallas_call | solution.py:471
  61.7 39.0 %combine.1 = (bf16[128,768]{1,0:T(8,128)(2,1)}, f32[8,128]{1,0:T(8,128)}) custom-call(bf16[288,2048]{1,0:T(8,128)(2,1)} %get-tuple-element.17.gd_ref, bf16[288,2048]{1,0:T(8,128)(2,1)} %get-tuple-element.18.ud_ref, bf16[3072,2048]{1,0:T(8,128)(2,1)} %wg_ref.3, bf16[3072,2048]{1,0:T(8,128)(2,1)} %wu_ref.3, bf16[512,288]{1,0:T(8,128)(2,1)} %get-tuple-element.19.place_ref, ...), custom_call_target="tpu_custom_call" | custom-call | tf_op jit(solution)/shard_map/combine/pallas_call | solution.py:520
  100.7 1.2 slice_bitcast_fusion
  101.9 24.9 %weight_grads.1 = (bf16[3072,2048]{1,0:T(8,128)(2,1)}, bf16[3072,2048]{1,0:T(8,128)(2,1)}, bf16[2048,3072]{1,0:T(8,128)(2,1)}) custom-call(bf16[288,3072]{1,0:T(8,128)(2,1)} %get-tuple-element.23.x_ref, bf16[288,2048]{1,0:T(8,128)(2,1)} %get-tuple-element.17.gd_ref, bf16[288,2048]{1,0:T(8,128)(2,1)} %get-tuple-element.18.ud_ref, ...), custom_call_target="tpu_custom_call" | custom-call | tf_op jit(solution)/shard_map/weight_grads/pallas_call | solution.py:584
  126.8 1.6 %copy.13 = bf16[128,768]{1,0:T(8,128)(2,1)} copy(bf16[128,768]{1,0:T(8,128)(2,1)} %get-tuple-element.34) | data formatting | bytes 393216
